TPU v7x, 256 devices: a whole 4x4x8 slice. The times are simulated.
256 devices in a mesh: cluster: 64 (over z, x_hi, y), species: 2 (over core), owner: 2 (over x_lo).
Axes of the slice: x: 4 (x_hi: 2, x_lo: 2; x = x_hi * 2 + x_lo), y: 4, z: 8, core: 2. Of those that a mesh axis runs over, the one named last changes fastest.
Arguments:
- state: float32 [4, 64, 512, 256], P('species', None, ('cluster', 'owner')), may hold values from -6 to 6
- near_blocks: bfloat16 [9, 256, 256], replicated, as said below
- basis: bfloat16 [256, 48], replicated, may hold values from -0.375 to 0.375
- leaf_tiles: float32 [40, 48, 48], replicated, may hold values from -0.125 to 0.125
- leaf_links: int32 [64, 512, 40], P(None, ('cluster', 'owner')), may hold values 0 or 1
- up_leaf: float32 [64, 8, 48, 48], P(None, 'owner'), may hold values from -0.0390625 to 0.0390625
- up_coarse: float32 [2, 64, 48, 48], replicated, may hold values from -0.625 to 0.625
- coarse_tiles: float32 [3, 64, 4, 48, 48], P(None, 'cluster', None, None, 'owner'), may hold values from -0.25 to 0.25
- coarse_links: int32 [3, 64, 4], P(None, 'cluster'), may hold values 0 or 1
- down_leaf: float32 [64, 8, 48, 48], P(None, 'owner'), may hold values from -0.875 to 0.875
- diffusion: float32 [4], P('species'), may hold values from 0.5 to 3
- speed: float32 [2, 64, 512, 256], P(None, None, ('cluster', 'owner')), may hold values from 0.5 to 4
- upwind: int32 [2, 64, 512, 256], P(None, None, ('cluster', 'owner')), may hold values from 0 to 1
- zone: int32 [64, 512, 256], P(None, ('cluster', 'owner')), may hold values from 0 to 15
- rate: float32 [16, 4, 4], replicated, may hold values from -6 to 6
Outputs:
- new_state: float32 [4, 64, 512, 256], P('species', None, ('cluster', 'owner'))
Inputs may be any that keep to these rules, and one draw needn't show every extreme that they name: The diagonal of the centre block near_blocks[4] lies between 1.8 and 6.2.
All inputs are finite; a program needn't handle non-finite values. No bound on the sum of `leaf_links` or of `coarse_links` on one device may be relied on, other than what follows from the above.
Results may differ from a plain program's by a relative error of at most 0.0021.
The roundings to bfloat16 on the way count: a program that leaves them out, or rounds other values in their place, can miss the bound.
Values may be sent and summed in bfloat16 or wider, within the bound.
A program may use at most 128 MiB of HBM per device.

v0:
```python
import jax
import jax.numpy as jnp
from jax import lax
from jax.experimental import pallas as pl
from jax.experimental.pallas import tpu as pltpu
from jax.sharding import PartitionSpec as P

F32 = jnp.float32
BF16 = jnp.bfloat16
I32 = jnp.int32
SWEEPS = 2
STEP = 0.1
RANK = 48
PY = 64
HIGHEST = lax.Precision.HIGHEST
NT = (((1,), (1,)), ((), ()))
TN = (((0,), (0,)), ((), ()))
NN = (((1,), (0,)), ((), ()))
FAR = [(dy, dx) for dy in range(-3, 4) for dx in range(-3, 4) if max(abs(dy), abs(dx)) >= 2]
GROUP_OFFSETS = (2, 3, -2, -3)
REACH = (-3, -2, -1, 1, 2, 3)


def dot(a, b, dims, precision=None):
    return lax.dot_general(a, b, dims, precision=precision, preferred_element_type=F32)


def lanes(shape):
    return lax.broadcasted_iota(I32, shape, len(shape) - 1)


def rows(shape):
    return lax.broadcasted_iota(I32, shape, len(shape) - 2)


def shift_rows_in_lanes(x, dy):
    if dy == 0:
        return x
    near = pltpu.roll(x, (-dy) % 128, 1)
    wrapped = pltpu.roll(x, (64 - dy) % 128, 1)
    at = lanes(x.shape) % 64 + dy
    return jnp.where((at >= 0) & (at < 64), near, wrapped)


def row_products(total, a_ref, w_ref, px):
    def block(i, acc):
        first = pl.multiple_of(i * 8, 8)
        a = a_ref[pl.ds(first, 8), :]
        for j in range(8):
            acc = acc + a[j : j + 1, :] * w_ref[px, first + j]
        return acc

    return lax.fori_loop(0, RANK // 8, block, total)


def kernel(
    state, near_blocks, basis_t, leaf_tiles, links, up_leaf, down_leaf, up_coarse, tiles, speed, upwind, zone,
    rate, coarse_links, diffusion,
    out,
    s0, cur, tgt, near_acc, low, oth, ctf, ctb, ctx, q, spd, upw, zon, nb, bt, lt, ltt, lk, msk, rhs,
    u_raw, u_dup, d_raw, d_dup, upc, upg, tcx, t2, tab, level, cfb, expd, p1, r2,
    load_sem, load8_sem, p1_send, p1_recv, r2_send, r2_recv, halo_send, halo_recv, one_send, one_recv,
):
    cluster = lax.axis_index("cluster")
    owner = lax.axis_index("owner")
    species = lax.axis_index("species")
    n_clusters = lax.axis_size("cluster")
    group = cluster // 4
    y0 = cluster % 4
    n_groups = n_clusters // 4
    slot = y0 * 2 + owner
    line = cluster * 2 + owner
    n_line = n_clusters * 2
    right = lax.rem(line + 1, n_line)
    left = lax.rem(line + n_line - 1, n_line)
    right_id = {"cluster": right // 2, "owner": right % 2}
    left_id = {"cluster": left // 2, "owner": left % 2}
    other_id = {"species": 1 - species}

    def ring_id(k):
        there = lax.rem(slot + k, 8)
        return {"cluster": group * 4 + there // 2, "owner": there % 2}

    def reach_id(d):
        return {"cluster": lax.rem(group + d + n_groups, n_groups) * 4 + y0}

    def load(src, dst, i):
        copy = pltpu.make_async_copy(src, dst, load_sem.at[i])
        copy.start()
        return copy

    state_loads = []
    for s in range(2):
        for px in range(4):
            copy = pltpu.make_async_copy(state.at[s, :, px], s0.at[px, pl.ds(64 * s, 64)], load8_sem.at[0, s * 4 + px])
            copy.start()
            state_loads.append(copy)
    bt_load = load(basis_t, bt, 0)
    flow_loads = []
    for j, (src, dst) in enumerate(((speed, spd), (upwind, upw))):
        for e in range(2):
            for px in range(4):
                copy = pltpu.make_async_copy(src.at[e, :, px], dst.at[e, px], load8_sem.at[1 + j, e * 4 + px])
                copy.start()
                flow_loads.append(copy)
    u_loads = [load(up_leaf.at[px], u_raw.at[px], 1 + px) for px in range(4)]
    tiles_load = load(tiles, tcx.at[:, :, owner], 5)
    zone_loads = []
    for px in range(4):
        copy = pltpu.make_async_copy(zone.at[:, px], zon.at[px], load8_sem.at[3, px])
        copy.start()
        zone_loads.append(copy)
    nb_load = load(near_blocks, nb, 6)
    lk_load = load(links, lk, 7)
    upc_load = load(up_coarse, upc, 8)
    lt_load = load(leaf_tiles, lt, 9)
    d_loads = [load(down_leaf.at[px], d_raw.at[px], 10 + px) for px in range(4)]

    r2[:, 7:] = jnp.zeros((SWEEPS, 9, 8, 128), F32)
    barrier = pltpu.get_barrier_semaphore()
    partners = [ring_id(k) for k in range(1, 8)] + [reach_id(d) for d in REACH] + [left_id, right_id, other_id]
    for partner in partners:
        pl.semaphore_signal(barrier, inc=1, device_id=partner, device_id_type=pl.DeviceIdType.MESH)

    def remote(src, dst, send, recv, device_id):
        return pltpu.make_async_remote_copy(
            src_ref=src, dst_ref=dst, send_sem=send, recv_sem=recv,
            device_id=device_id, device_id_type=pl.DeviceIdType.MESH,
        )

    scale_0 = STEP * diffusion[0]
    scale_1 = STEP * diffusion[1]
    scale = jnp.where(lax.broadcasted_iota(I32, (128, 1), 0) < 64, scale_0, scale_1)

    tab[...] = jnp.zeros_like(tab)

    def own_columns(k, src):
        def column(px, _):
            v = src[px].astype(BF16)
            low[k, px + 1] = v
            coeffs = dot(bt[...], v, NT)
            ctf[px] = coeffs
            ctb[k, px + 3] = coeffs.astype(BF16)
            return 0

        lax.fori_loop(0, 4, column, 0)

    def halo_copies(k):
        h, g = halo_send, halo_recv
        return [
            remote(low.at[k, 4], low.at[k, 0], h.at[k, 0], g.at[k, 0], right_id),
            remote(low.at[k, 1], low.at[k, 5], h.at[k, 1], g.at[k, 1], left_id),
            remote(ctb.at[k, pl.ds(4, 3)], ctb.at[k, pl.ds(0, 3)], h.at[k, 2], g.at[k, 2], right_id),
            remote(ctb.at[k, pl.ds(3, 3)], ctb.at[k, pl.ds(7, 3)], h.at[k, 3], g.at[k, 3], left_id),
        ]

    def root_tile(total):
        pick_row = rows((8, 128)) - 2 * y0
        pick = jnp.where((pick_row >= 0) & (pick_row < 2) & (lanes((8, 128)) // 64 == pick_row), 1.0, 0.0)
        padded = jnp.concatenate([total, jnp.zeros((128 - RANK, 128), F32)], axis=0)
        return dot(pick, padded, NT, HIGHEST)

    def send_roots(k, total):
        p1[k, 0] = root_tile(total)
        copies = [remote(p1.at[k, 0], p1.at[k, j], p1_send.at[k, j], p1_recv.at[k, j], ring_id(j)) for j in range(1, 8)]
        for copy in copies:
            copy.start()
        return copies

    def send_groups(k, copies):
        for copy in copies:
            copy.wait_recv()
        tile = p1[k, 0]
        for j in range(1, 8):
            tile = tile + p1[k, j]
        r2[k, 3] = tile
        sends = [
            remote(r2.at[k, 3], r2.at[k, 3 - d], r2_send.at[k, 3 + d], r2_recv.at[k, 3 + d], reach_id(d)) for d in REACH
        ]
        for copy in sends:
            copy.start()
        return sends

    def near(k):
        for dy in (0, -1, 1):
            wide = jnp.concatenate([low[k, dx + 1 : dx + 5].reshape(512, 256) for dx in (-1, 0, 1)], axis=1)
            at = 3 * (dy + 1)
            part = dot(wide, nb[at : at + 3].reshape(768, 256), NN)
            for b in range(8):
                block = part[64 * b : 64 * b + 64]
                px, s = b // 2, b % 2
                if dy == 0:
                    near_acc[px, pl.ds(64 * s, 64)] = block
                else:
                    near_acc[px, pl.ds(64 * s, 64)] += pltpu.roll(block, (-dy) % 64, 0)

    def leaf(k):
        def widen(px, _):
            ctx[px] = ctb[k, px].astype(F32)
            return 0

        lax.fori_loop(0, 10, widen, 0)
        first = 0
        for dy in range(-3, 4):
            mine = [dx for y, dx in FAR if y == dy]
            n = len(mine)

            def stack(px, _, mine=mine, first=first):
                for i, dx in enumerate(mine):
                    masked = ctx[px + 3 + dx] * msk[px, first + i : first + i + 1, :]
                    rhs[px, pl.ds(i * RANK, RANK), :] = masked.astype(BF16)
                return 0

            lax.fori_loop(0, 4, stack, 0)
            for px in range(4):
                part = dot(ltt[:, first * RANK : (first + n) * RANK], rhs[px, : n * RANK, :], NN)
                part = shift_rows_in_lanes(part, dy)
                if first == 0:
                    expd[px] = part
                else:
                    expd[px] += part
            first += n

    def prepare_masks():
        for px in range(4):
            both = jnp.concatenate([lk[px].astype(F32)] * 2, axis=1)
            first = 0
            for dy in range(-3, 4):
                n = sum(1 for y, _ in FAR if y == dy)
                msk[px, first : first + n, :] = shift_rows_in_lanes(both[first : first + n], -dy)
                first += n

    def prepare_leaf_tiles():
        first = 0
        for dy in range(-3, 4):
            n = sum(1 for y, _ in FAR if y == dy)
            stacked = lt[first : first + n].reshape(n * RANK, RANK)
            ltt[:, first * RANK : (first + n) * RANK] = jnp.swapaxes(stacked, 0, 1).astype(BF16)
            first += n

    def prepare_coarse():
        lane = lanes((64, 128))
        at_group = group + lane // 8 - 3 + n_groups
        at_y = (lane // 2) % 4
        for i, target in enumerate(((4 * at_group + at_y) % n_clusters, (2 * at_group + at_y // 2) % (n_clusters // 2))):
            pick = jnp.where((rows((64, 128)) == target) & (lane < 56), 1.0, 0.0).astype(BF16)

            def block(b, _, pick=pick, i=i):
                x = upc[i, pl.ds(b * 8, 8)].reshape(8 * RANK, 64)
                high = x.astype(BF16)
                rest = (x - high.astype(F32)).astype(BF16)
                upg[i, pl.ds(b * 8, 8)] = (dot(high, pick, NN) + dot(rest, pick, NN)).reshape(8, RANK, 128)
                return 0

            lax.fori_loop(0, RANK // 8, block, 0)
        for l in range(3):
            for k in range(4):
                at = (l * 4 + k) * RANK
                t2[:, at : at + RANK] = tcx[l, k].reshape(RANK, RANK)

    def coarse(k):
        zero = jnp.zeros((RANK, 128), F32)
        lane = lanes((1, 128))
        at_d, at_y = lane // 8 - 3, (lane // 2) % 4
        wide_lane = lanes((RANK, 128))
        values = jnp.swapaxes(r2[k].reshape(128, 128), 0, 1)[:RANK]
        pieces = []
        for l in range(3):
            if l > 0:
                level[...] = values
                raised = row_products(zero, level, upg, l - 1)
                hop = 2 * l
                sibling = jnp.where((wide_lane // hop) % 2 == 0, pltpu.roll(raised, 128 - hop, 1), pltpu.roll(raised, hop, 1))
                values = raised + sibling
            for i, offset in enumerate(GROUP_OFFSETS):
                if l == 0:
                    hit = at_d * 4 + at_y == y0 + offset
                elif l == 1:
                    hit = (at_d * 2 + at_y // 2 == y0 // 2 + offset) & (at_y % 2 == 0)
                else:
                    hit = (at_d == offset) & (at_y == 0)
                hit = hit & (lane < 56)
                pieces.append(values * jnp.where(hit, coarse_links[l, 0, i].astype(F32), 0.0))
        found = dot(t2[...], jnp.concatenate(pieces, axis=0), NN, HIGHEST)
        spread = jnp.where(rows((128, 128)) % 2 == lanes((128, 128)) // 64, 1.0, 0.0)
        cfb[...] = dot(found, spread, NN, HIGHEST)

    def finish(k, src, dst, inverse_diag):
        def column(px, _):
            field = row_products(expd[px], cfb, d_dup, px).astype(BF16)
            applied = near_acc[px] + dot(field, bt[...], TN)
            v = src[px]
            dst[px] = v + (tgt[px] - v - scale * applied) * inverse_diag
            return 0

        lax.fori_loop(0, 4, column, 0)

    def reaction(px, _):
        z = zon[px]
        values = [jnp.tanh(s0[px, :64]), jnp.tanh(s0[px, 64:])]
        there = oth[px].astype(F32)
        values += [jnp.tanh(there[:64]), jnp.tanh(there[64:])]
        for s in range(2):
            total = jnp.zeros((64, 256), F32)
            for t in range(4):
                table = jnp.broadcast_to(tab[4 * s + t : 4 * s + t + 1, :], (64, 128))
                found = [jnp.take_along_axis(table, z[:, h : h + 128], axis=1) for h in (0, 128)]
                total = total + jnp.concatenate(found, axis=1) * values[t]
            tgt[px, pl.ds(64 * s, 64)] = s0[px, pl.ds(64 * s, 64)] + STEP * total
        return 0

    def advection(s, _):
        at = pl.ds(pl.multiple_of(s * 64, 64), 64)
        n = lanes((64, 256))

        def flux_x(px):
            v = low[0, px + 1, at].astype(F32)
            before = low[0, px, at].astype(F32)
            v_left = pltpu.roll(jnp.where(n % 16 == 15, pltpu.roll(before, 256 - 16, 1), v), 1, 1)
            w = q[0, px]
            return v, w * jnp.where(w > 0, v_left, v)

        v, flux = flux_x(0)
        for px in range(4):
            v_next, flux_next = flux_x(px + 1)
            flux_right = pltpu.roll(jnp.where(n % 16 == 0, pltpu.roll(flux_next, 16, 1), flux), 255, 1)
            v_up = pltpu.roll(jnp.where(n >= 240, pltpu.roll(v, 1, 0), v), 16, 1)
            w = q[1, px]
            flux_y = w * jnp.where(w > 0, v_up, v)
            flux_down = pltpu.roll(jnp.where(n < 16, pltpu.roll(flux_y, 63, 0), flux_y), 256 - 16, 1)
            tgt[px, at] += STEP * (flux - flux_right + flux_y - flux_down)
            v, flux = v_next, flux_next
        return 0

    for copy in state_loads:
        copy.wait()
    bt_load.wait()
    own_columns(0, s0)
    pl.semaphore_wait(barrier, len(partners))
    halos = halo_copies(0)
    others = remote(low.at[0, pl.ds(1, 4)], oth, one_send.at[0], one_recv.at[0], other_id)
    for copy in halos:
        copy.start()
    others.start()
    tiles_load.wait()
    tile_copy = remote(tcx.at[:, :, owner], tcx.at[:, :, owner], one_send.at[1], one_recv.at[1], {"owner": 1 - owner})
    tile_copy.start()
    for copy in flow_loads:
        copy.wait()

    def signed(px, _):
        for e in range(2):
            v = spd[e, px]
            q[e, px] = jnp.where(upw[e, px] == 0, v, -v)
        return 0

    lax.fori_loop(0, 4, signed, 0)
    edge = remote(q.at[0, 0], q.at[0, 4], one_send.at[2], one_recv.at[2], left_id)
    edge.start()

    for copy in u_loads:
        copy.wait()

    def doubled(raw, dup):
        def block(i, _):
            x = raw[i // RANK, i % RANK]
            dup[i // RANK, i % RANK] = jnp.concatenate([x, x], axis=1)
            return 0

        lax.fori_loop(0, 4 * RANK, block, 0, unroll=8)

    doubled(u_raw, u_dup)

    def roots():
        total = jnp.zeros((RANK, 128), F32)
        for px in range(4):
            total = row_products(total, ctf.at[px], u_dup, px)
        return total

    ring = send_roots(0, roots())

    for s in range(2):
        for t in range(4):
            at = (2 * species + t) % 4
            tab[4 * s + t : 4 * s + t + 1, :16] = rate[2 * species + s, pl.ds(at, 1), :]
    for copy in zone_loads:
        copy.wait()
    others.wait_recv()
    lax.fori_loop(0, 4, reaction, 0)

    reach = send_groups(0, ring)
    for copy in halos:
        copy.wait_recv()
    edge.wait_recv()
    lax.fori_loop(0, 2, advection, 0)
    nb_load.wait()
    near(0)
    eye = rows((256, 256)) == lanes((256, 256))
    diag = jnp.sum(jnp.where(eye, nb[4].astype(F32), 0.0), axis=0, keepdims=True)
    inverse_diag = 1.0 / (1.0 + scale * diag)
    lk_load.wait()
    prepare_masks()
    lt_load.wait()
    prepare_leaf_tiles()
    leaf(0)
    upc_load.wait()
    tile_copy.wait_recv()
    prepare_coarse()
    for copy in d_loads:
        copy.wait()
    doubled(d_raw, d_dup)
    for copy in reach:
        copy.wait_recv()
    coarse(0)
    finish(0, s0, cur, inverse_diag)

    own_columns(1, cur)
    halos_1 = halo_copies(1)
    for copy in halos_1:
        copy.start()
    ring_1 = send_roots(1, roots())
    for copy in halos_1:
        copy.wait_recv()
    near(1)
    reach_1 = send_groups(1, ring_1)
    leaf(1)
    for copy in reach_1:
        copy.wait_recv()
    coarse(1)
    finish(1, cur, out, inverse_diag)

    for copy in halos + halos_1 + [others, tile_copy, edge] + ring + ring_1 + reach + reach_1:
        copy.wait_send()


def per_device(
    state, near_blocks, basis, leaf_tiles, leaf_links, up_leaf, up_coarse, coarse_tiles, coarse_links,
    down_leaf, diffusion, speed, upwind, zone, rate,
):
    anywhere = pl.BlockSpec(memory_space=pl.ANY)
    vmem = pl.BlockSpec(memory_space=pltpu.VMEM)
    smem = pl.BlockSpec(memory_space=pltpu.SMEM)
    dma = pltpu.SemaphoreType.DMA
    scratch = [
        pltpu.VMEM((4, 128, 256), F32),
        pltpu.VMEM((4, 128, 256), F32),
        pltpu.VMEM((4, 128, 256), F32),
        pltpu.VMEM((4, 128, 256), F32),
        pltpu.VMEM((2, 6, 128, 256), BF16),
        pltpu.VMEM((4, 128, 256), BF16),
        pltpu.VMEM((4, RANK, 128), F32),
        pltpu.VMEM((2, 10, RANK, 128), BF16),
        pltpu.VMEM((10, RANK, 128), F32),
        pltpu.VMEM((2, 5, 64, 256), F32),
        pltpu.VMEM((2, 4, 64, 256), F32),
        pltpu.VMEM((2, 4, 64, 256), I32),
        pltpu.VMEM((4, 64, 256), I32),
        pltpu.VMEM((9, 256, 256), BF16),
        pltpu.VMEM((RANK, 256), BF16),
        pltpu.VMEM((40, RANK, RANK), F32),
        pltpu.VMEM((RANK, 40 * RANK), BF16),
        pltpu.VMEM((4, 40, 64), I32),
        pltpu.VMEM((4, 40, 128), F32),
        pltpu.VMEM((4, 7 * RANK, 128), BF16),
        pltpu.VMEM((4, RANK, RANK, 64), F32),
        pltpu.VMEM((4, RANK, RANK, 128), F32),
        pltpu.VMEM((4, RANK, RANK, 64), F32),
        pltpu.VMEM((4, RANK, RANK, 128), F32),
        pltpu.VMEM((2, RANK, RANK, 64), F32),
        pltpu.VMEM((2, RANK, RANK, 128), F32),
        pltpu.VMEM((3, 4, 2, 24, RANK), F32),
        pltpu.VMEM((RANK, 12 * RANK), F32),
        pltpu.VMEM((8, 128), F32),
        pltpu.VMEM((RANK, 128), F32),
        pltpu.VMEM((RANK, 128), F32),
        pltpu.VMEM((4, RANK, 128), F32),
        pltpu.VMEM((2, 8, 8, 128), F32),
        pltpu.VMEM((2, 16, 8, 128), F32),
        dma((14,)),
        dma((4, 8)),
        dma((2, 8)),
        dma((2, 8)),
        dma((2, 7)),
        dma((2, 7)),
        dma((2, 4)),
        dma((2, 4)),
        dma((3,)),
        dma((3,)),
    ]
    result = pl.pallas_call(
        kernel,
        out_shape=jax.ShapeDtypeStruct((4, 128, 256), F32),
        in_specs=[anywhere] * 12 + [vmem, smem, smem],
        out_specs=vmem,
        scratch_shapes=scratch,
        compiler_params=pltpu.CompilerParams(
            collective_id=0, has_side_effects=True, vmem_limit_bytes=56 * 1024 * 1024
        ),
    )(
        state,
        near_blocks,
        basis.T,
        leaf_tiles,
        jnp.transpose(leaf_links, (1, 2, 0)),
        jnp.transpose(up_leaf, (1, 2, 3, 0)),
        jnp.transpose(down_leaf, (1, 2, 3, 0)),
        jnp.transpose(up_coarse, (0, 2, 3, 1)),
        jnp.transpose(coarse_tiles[:, 0], (0, 1, 3, 2)),
        speed,
        upwind,
        zone,
        jnp.transpose(rate, (1, 2, 0)),
        coarse_links,
        diffusion,
    )
    return jnp.transpose(result.reshape(4, 2, PY, 256), (1, 2, 0, 3))


def solution(mesh):
    return jax.shard_map(
        per_device,
        mesh=mesh,
        in_specs=(
            P("species", None, ("cluster", "owner"), None),
            P(),
            P(),
            P(),
            P(None, ("cluster", "owner"), None),
            P(None, "owner", None, None),
            P(),
            P(None, "cluster", None, None, "owner"),
            P(None, "cluster", None),
            P(None, "owner", None, None),
            P("species"),
            P(None, None, ("cluster", "owner"), None),
            P(None, None, ("cluster", "owner"), None),
            P(None, ("cluster", "owner"), None),
            P(),
        ),
        out_specs=P("species", None, ("cluster", "owner"), None),
        check_vma=False,
    )
```

profile of v0, /device:TPU:2, one launch (start us, length us, event | category | flops | bytes accessed | tf_op | source)
XLA Modules:
  0.0 52.8 jit_solution(8420325254649237507)
XLA Ops:
  0.0 50.6 %shard_map.145 = f32[4,128,256]{2,1,0:T(8,128)} custom-call(f32[2,64,4,256]{3,2,1,0:T(4,128)} %state.1, bf16[9,256,256]{2,1,0:T(8,128)(2,1)} %near_blocks.1, bf16[48,256]{1,0:T(8,128)(2,1)} %bitcast.19, f32[40,48,48]{2,1,0:T(8,128)} %leaf_tiles.1, s32[4,40,64]{2,1,0:T(8,128)} %bitcast.18, f32[4,48,48,64]{3,2,1,0:T(8,128)} %bitcast.13, ...), custom_call_target="tpu_custom_call" | custom-call | tf_op jit(solution)/shard_map/pallas_call | solution.py:490
  50.7 2.2 %copy.18 = f32[4,2,64,256]{3,0,2,1:T(4,128)} copy(f32[4,2,64,256]{3,2,1,0:T(8,128)} %bitcast.16) | data formatting | bytes 1048576 | tf_op jit(solution)/shard_map/reshape | solution.py:516
where the time goes:
time: 53.1 us; the launch traced here: 52.8 us
  Pallas kernels  50.6 us (95%)
  local copies, waits for them, and re-layouts  2.17 us (4%)
    pallas_call x1, Pallas kernels, per_device(): pl.pallas_call(kernel, out_shape=jax.ShapeDtypeStruct((4, 128, 256), F32)...  50.6 us
    reshape x1, local copies, waits for them, and re-layouts, per_device(): return jnp.transpose(result.reshape(4, 2, PY, 256), (1, 2, 0, 3))  2.17 us

commit v1 on v0

--- a/solution.py
+++ b/solution.py
@@ -18,7 +18,7 @@
 NN = (((1,), (0,)), ((), ()))
 FAR = [(dy, dx) for dy in range(-3, 4) for dx in range(-3, 4) if max(abs(dy), abs(dx)) >= 2]
 GROUP_OFFSETS = (2, 3, -2, -3)
-REACH = (-3, -2, -1, 1, 2, 3)
+REACH = [(d, o) for d in (-3, 3, -2, 2, -1, 1) for o in (0, 1)] + [(0, 1)]
 
 
 def dot(a, b, dims, precision=None):
@@ -42,23 +42,34 @@
     return jnp.where((at >= 0) & (at < 64), near, wrapped)
 
 
-def row_products(total, a_ref, w_ref, px):
-    def block(i, acc):
-        first = pl.multiple_of(i * 8, 8)
-        a = a_ref[pl.ds(first, 8), :]
-        for j in range(8):
-            acc = acc + a[j : j + 1, :] * w_ref[px, first + j]
-        return acc
-
-    return lax.fori_loop(0, RANK // 8, block, total)
+def split_dot(a, b, dims, exact):
+    whole = b if exact == 0 else a
+    high = whole.astype(BF16)
+    rest = (whole - high.astype(F32)).astype(BF16)
+    if exact == 0:
+        return dot(a, high, dims) + dot(a, rest, dims)
+    return dot(high, b, dims) + dot(rest, b, dims)
+
+
+def row_products(total, a, w_ref, at):
+    for r in range(RANK):
+        total = total + a[r : r + 1, :] * w_ref[at, r]
+    return total
+
+
+def both_products(totals, left, w_ref, at):
+    for r in range(RANK):
+        w = w_ref[at, r]
+        totals = tuple(total + a[r : r + 1, :] * w for total, a in zip(totals, left))
+    return totals
 
 
 def kernel(
     state, near_blocks, basis_t, leaf_tiles, links, up_leaf, down_leaf, up_coarse, tiles, speed, upwind, zone,
     rate, coarse_links, diffusion,
     out,
-    s0, cur, tgt, near_acc, low, oth, ctf, ctb, ctx, q, spd, upw, zon, nb, bt, lt, ltt, lk, msk, rhs,
-    u_raw, u_dup, d_raw, d_dup, upc, upg, tcx, t2, tab, level, cfb, expd, p1, r2,
+    s0, cur, tgt, near_acc, low, oth, ctf, ctb, q, spd, upw, zon, nb, bt, lt, ltt, lk, msk, rhs,
+    u_raw, d_raw, upc, upg, tcx, t2, tab, cfb, expd, fld, p1, r2,
     load_sem, load8_sem, p1_send, p1_recv, r2_send, r2_recv, halo_send, halo_recv, one_send, one_recv,
 ):
     cluster = lax.axis_index("cluster")
@@ -68,7 +79,6 @@
     group = cluster // 4
     y0 = cluster % 4
     n_groups = n_clusters // 4
-    slot = y0 * 2 + owner
     line = cluster * 2 + owner
     n_line = n_clusters * 2
     right = lax.rem(line + 1, n_line)
@@ -78,11 +88,16 @@
     other_id = {"species": 1 - species}
 
     def ring_id(k):
-        there = lax.rem(slot + k, 8)
-        return {"cluster": group * 4 + there // 2, "owner": there % 2}
-
-    def reach_id(d):
-        return {"cluster": lax.rem(group + d + n_groups, n_groups) * 4 + y0}
+        return {"cluster": group * 4 + lax.rem(y0 + k, 4)}
+
+    def reach_id(d, o):
+        return {"cluster": lax.rem(group + d + n_groups, n_groups) * 4 + y0, "owner": lax.rem(owner + o, 2)}
+
+    r2[:, :, 7:] = jnp.zeros((SWEEPS, 2, 9, 8, 128), F32)
+    barrier = pltpu.get_barrier_semaphore()
+    partners = [ring_id(k) for k in (1, 2, 3)] + [reach_id(d, o) for d, o in REACH] + [left_id, right_id, other_id]
+    for partner in partners:
+        pl.semaphore_signal(barrier, inc=1, device_id=partner, device_id_type=pl.DeviceIdType.MESH)
 
     def load(src, dst, i):
         copy = pltpu.make_async_copy(src, dst, load_sem.at[i])
@@ -96,6 +111,7 @@
             copy.start()
             state_loads.append(copy)
     bt_load = load(basis_t, bt, 0)
+    u_loads = [load(up_leaf.at[px], u_raw.at[px], 1 + px) for px in range(4)]
     flow_loads = []
     for j, (src, dst) in enumerate(((speed, spd), (upwind, upw))):
         for e in range(2):
@@ -103,24 +119,17 @@
                 copy = pltpu.make_async_copy(src.at[e, :, px], dst.at[e, px], load8_sem.at[1 + j, e * 4 + px])
                 copy.start()
                 flow_loads.append(copy)
-    u_loads = [load(up_leaf.at[px], u_raw.at[px], 1 + px) for px in range(4)]
     tiles_load = load(tiles, tcx.at[:, :, owner], 5)
+    lk_load = load(links, lk, 7)
+    upc_load = load(up_coarse, upc, 8)
+    lt_load = load(leaf_tiles, lt, 9)
     zone_loads = []
     for px in range(4):
         copy = pltpu.make_async_copy(zone.at[:, px], zon.at[px], load8_sem.at[3, px])
         copy.start()
         zone_loads.append(copy)
     nb_load = load(near_blocks, nb, 6)
-    lk_load = load(links, lk, 7)
-    upc_load = load(up_coarse, upc, 8)
-    lt_load = load(leaf_tiles, lt, 9)
     d_loads = [load(down_leaf.at[px], d_raw.at[px], 10 + px) for px in range(4)]
-
-    r2[:, 7:] = jnp.zeros((SWEEPS, 9, 8, 128), F32)
-    barrier = pltpu.get_barrier_semaphore()
-    partners = [ring_id(k) for k in range(1, 8)] + [reach_id(d) for d in REACH] + [left_id, right_id, other_id]
-    for partner in partners:
-        pl.semaphore_signal(barrier, inc=1, device_id=partner, device_id_type=pl.DeviceIdType.MESH)
 
     def remote(src, dst, send, recv, device_id):
         return pltpu.make_async_remote_copy(
@@ -135,15 +144,13 @@
     tab[...] = jnp.zeros_like(tab)
 
     def own_columns(k, src):
-        def column(px, _):
+        for px in range(4):
             v = src[px].astype(BF16)
             low[k, px + 1] = v
             coeffs = dot(bt[...], v, NT)
-            ctf[px] = coeffs
+            ctf[0, px] = coeffs[:, :64]
+            ctf[1, px] = coeffs[:, 64:]
             ctb[k, px + 3] = coeffs.astype(BF16)
-            return 0
-
-        lax.fori_loop(0, 4, column, 0)
 
     def halo_copies(k):
         h, g = halo_send, halo_recv
@@ -156,13 +163,12 @@
 
     def root_tile(total):
         pick_row = rows((8, 128)) - 2 * y0
-        pick = jnp.where((pick_row >= 0) & (pick_row < 2) & (lanes((8, 128)) // 64 == pick_row), 1.0, 0.0)
+        pick = jnp.where((pick_row >= 0) & (pick_row < 2) & (lanes((8, 128)) // 64 == pick_row), 1.0, 0.0).astype(BF16)
         padded = jnp.concatenate([total, jnp.zeros((128 - RANK, 128), F32)], axis=0)
-        return dot(pick, padded, NT, HIGHEST)
-
-    def send_roots(k, total):
-        p1[k, 0] = root_tile(total)
-        copies = [remote(p1.at[k, 0], p1.at[k, j], p1_send.at[k, j], p1_recv.at[k, j], ring_id(j)) for j in range(1, 8)]
+        return split_dot(pick, padded, NT, 0)
+
+    def send_roots(k):
+        copies = [remote(p1.at[k, 0], p1.at[k, j], p1_send.at[k, j], p1_recv.at[k, j], ring_id(j)) for j in (2, 1, 3)]
         for copy in copies:
             copy.start()
         return copies
@@ -171,64 +177,65 @@
         for copy in copies:
             copy.wait_recv()
         tile = p1[k, 0]
-        for j in range(1, 8):
+        for j in (1, 2, 3):
             tile = tile + p1[k, j]
-        r2[k, 3] = tile
+        r2[k, 0, 3] = tile
         sends = [
-            remote(r2.at[k, 3], r2.at[k, 3 - d], r2_send.at[k, 3 + d], r2_recv.at[k, 3 + d], reach_id(d)) for d in REACH
+            remote(r2.at[k, 0, 3], r2.at[k, o, 3 - d], r2_send.at[k, i], r2_recv.at[k, i], reach_id(d, o))
+            for i, (d, o) in enumerate(REACH)
         ]
         for copy in sends:
             copy.start()
         return sends
 
-    def near(k):
+    def near(k, columns):
         for dy in (0, -1, 1):
-            wide = jnp.concatenate([low[k, dx + 1 : dx + 5].reshape(512, 256) for dx in (-1, 0, 1)], axis=1)
+            wide = jnp.concatenate(
+                [jnp.concatenate([low[k, px + dx + 1] for px in columns], axis=0) for dx in (-1, 0, 1)], axis=1
+            )
             at = 3 * (dy + 1)
             part = dot(wide, nb[at : at + 3].reshape(768, 256), NN)
-            for b in range(8):
-                block = part[64 * b : 64 * b + 64]
-                px, s = b // 2, b % 2
-                if dy == 0:
-                    near_acc[px, pl.ds(64 * s, 64)] = block
-                else:
-                    near_acc[px, pl.ds(64 * s, 64)] += pltpu.roll(block, (-dy) % 64, 0)
+            for b, px in enumerate(columns):
+                for s in range(2):
+                    block = part[128 * b + 64 * s : 128 * b + 64 * s + 64]
+                    if dy == 0:
+                        near_acc[px, pl.ds(64 * s, 64)] = block
+                    else:
+                        near_acc[px, pl.ds(64 * s, 64)] += pltpu.roll(block, (-dy) % 64, 0)
 
     def leaf(k):
-        def widen(px, _):
-            ctx[px] = ctb[k, px].astype(F32)
-            return 0
-
-        lax.fori_loop(0, 10, widen, 0)
         first = 0
         for dy in range(-3, 4):
             mine = [dx for y, dx in FAR if y == dy]
             n = len(mine)
-
-            def stack(px, _, mine=mine, first=first):
+            side = (dy + 3) % 2
+            for px in range(4):
                 for i, dx in enumerate(mine):
-                    masked = ctx[px + 3 + dx] * msk[px, first + i : first + i + 1, :]
-                    rhs[px, pl.ds(i * RANK, RANK), :] = masked.astype(BF16)
-                return 0
-
-            lax.fori_loop(0, 4, stack, 0)
+                    coeffs = ctb[k, px + 3 + dx].reshape(3, 16, 128)
+                    masked = coeffs * msk[px, first + i][None]
+                    rhs[side, pl.ds(i * RANK, RANK), pl.ds(px * 128, 128)] = masked.reshape(RANK, 128)
+            part = dot(ltt[:, first * RANK : (first + n) * RANK], rhs[side, : n * RANK, :], NN)
             for px in range(4):
-                part = dot(ltt[:, first * RANK : (first + n) * RANK], rhs[px, : n * RANK, :], NN)
-                part = shift_rows_in_lanes(part, dy)
+                piece = shift_rows_in_lanes(part[:, px * 128 : px * 128 + 128], dy)
                 if first == 0:
-                    expd[px] = part
+                    expd[px] = piece
                 else:
-                    expd[px] += part
+                    expd[px] += piece
             first += n
 
     def prepare_masks():
-        for px in range(4):
+        def column(px, _):
             both = jnp.concatenate([lk[px].astype(F32)] * 2, axis=1)
             first = 0
             for dy in range(-3, 4):
                 n = sum(1 for y, _ in FAR if y == dy)
-                msk[px, first : first + n, :] = shift_rows_in_lanes(both[first : first + n], -dy)
+                turned = shift_rows_in_lanes(both[first : first + n], -dy)
+                for i in range(n):
+                    msk[px, first + i] = jnp.broadcast_to(turned[i : i + 1], (16, 128)).astype(BF16)
                 first += n
+            return 0
+
+        lax.fori_loop(0, 4, column, 0)
 
     def prepare_leaf_tiles():
         first = 0
@@ -246,29 +253,31 @@
             pick = jnp.where((rows((64, 128)) == target) & (lane < 56), 1.0, 0.0).astype(BF16)
 
             def block(b, _, pick=pick, i=i):
-                x = upc[i, pl.ds(b * 8, 8)].reshape(8 * RANK, 64)
-                high = x.astype(BF16)
-                rest = (x - high.astype(F32)).astype(BF16)
-                upg[i, pl.ds(b * 8, 8)] = (dot(high, pick, NN) + dot(rest, pick, NN)).reshape(8, RANK, 128)
+                x = upc[i, pl.ds(b * 8, 8)].reshape(8 * RANK, 64).astype(BF16)
+                upg[i, pl.ds(b * 8, 8)] = dot(x, pick, NN).reshape(8, RANK, 128)
                 return 0
 
             lax.fori_loop(0, RANK // 8, block, 0)
+    def prepare_coarse_tiles():
+        t2[...] = jnp.zeros_like(t2)
         for l in range(3):
             for k in range(4):
-                at = (l * 4 + k) * RANK
-                t2[:, at : at + RANK] = tcx[l, k].reshape(RANK, RANK)
+                at = (l * 4 + k) * 64
+                whole = tcx[l, k].reshape(RANK, RANK)
+                high = whole.astype(BF16)
+                t2[0, :, at : at + RANK] = high
+                t2[1, :, at : at + RANK] = (whole - high.astype(F32)).astype(BF16)
 
     def coarse(k):
         zero = jnp.zeros((RANK, 128), F32)
         lane = lanes((1, 128))
         at_d, at_y = lane // 8 - 3, (lane // 2) % 4
         wide_lane = lanes((RANK, 128))
-        values = jnp.swapaxes(r2[k].reshape(128, 128), 0, 1)[:RANK]
+        values = jnp.swapaxes((r2[k, 0] + r2[k, 1]).reshape(128, 128), 0, 1)[:RANK]
         pieces = []
         for l in range(3):
             if l > 0:
-                level[...] = values
-                raised = row_products(zero, level, upg, l - 1)
+                raised = row_products(zero, values, upg, l - 1)
                 hop = 2 * l
                 sibling = jnp.where((wide_lane // hop) % 2 == 0, pltpu.roll(raised, 128 - hop, 1), pltpu.roll(raised, hop, 1))
                 values = raised + sibling
@@ -281,19 +290,28 @@
                     hit = (at_d == offset) & (at_y == 0)
                 hit = hit & (lane < 56)
                 pieces.append(values * jnp.where(hit, coarse_links[l, 0, i].astype(F32), 0.0))
-        found = dot(t2[...], jnp.concatenate(pieces, axis=0), NN, HIGHEST)
-        spread = jnp.where(rows((128, 128)) % 2 == lanes((128, 128)) // 64, 1.0, 0.0)
-        cfb[...] = dot(found, spread, NN, HIGHEST)
-
-    def finish(k, src, dst, inverse_diag):
-        def column(px, _):
-            field = row_products(expd[px], cfb, d_dup, px).astype(BF16)
-            applied = near_acc[px] + dot(field, bt[...], TN)
+                pieces.append(jnp.zeros((16, 128), F32))
+        stacked = jnp.concatenate(pieces, axis=0)
+        high = stacked.astype(BF16)
+        rest = (stacked - high.astype(F32)).astype(BF16)
+        found = dot(t2[0], high, NN) + (dot(t2[0], rest, NN) + dot(t2[1], high, NN))
+        spread = jnp.where(rows((128, 256)) % 2 == lanes((128, 256)) // 128, 1.0, 0.0).astype(BF16)
+        both = split_dot(found, spread, NN, 1)
+        cfb[0] = both[:, :64]
+        cfb[1] = both[:, 128:192]
+
+    def finish(src, dst, inverse_diag):
+        def expand(px, _):
+            zero = jnp.zeros((RANK, 64), F32)
+            expanded = both_products((zero, zero), (cfb[0], cfb[1]), d_raw, px)
+            fld[px] = (expd[px] + jnp.concatenate(expanded, axis=1)).astype(BF16)
+            return 0
+
+        lax.fori_loop(0, 4, expand, 0)
+        for px in range(4):
+            applied = near_acc[px] + dot(fld[px], bt[...], TN)
             v = src[px]
             dst[px] = v + (tgt[px] - v - scale * applied) * inverse_diag
-            return 0
-
-        lax.fori_loop(0, 4, column, 0)
 
     def reaction(px, _):
         z = zon[px]
@@ -336,15 +354,23 @@
         copy.wait()
     bt_load.wait()
     own_columns(0, s0)
+    for copy in u_loads:
+        copy.wait()
+
+    def roots():
+        totals = lax.fori_loop(
+            0, 4, lambda px, t: both_products(t, (ctf[0, px], ctf[1, px]), u_raw, px), (jnp.zeros((RANK, 64), F32),) * 2
+        )
+        return jnp.concatenate(totals, axis=1)
+
+    p1[0, 0] = root_tile(roots())
     pl.semaphore_wait(barrier, len(partners))
+    ring = send_roots(0)
     halos = halo_copies(0)
     others = remote(low.at[0, pl.ds(1, 4)], oth, one_send.at[0], one_recv.at[0], other_id)
     for copy in halos:
         copy.start()
     others.start()
-    tiles_load.wait()
-    tile_copy = remote(tcx.at[:, :, owner], tcx.at[:, :, owner], one_send.at[1], one_recv.at[1], {"owner": 1 - owner})
-    tile_copy.start()
     for copy in flow_loads:
         copy.wait()
 
@@ -357,27 +383,17 @@
     lax.fori_loop(0, 4, signed, 0)
     edge = remote(q.at[0, 0], q.at[0, 4], one_send.at[2], one_recv.at[2], left_id)
     edge.start()
-
-    for copy in u_loads:
-        copy.wait()
-
-    def doubled(raw, dup):
-        def block(i, _):
-            x = raw[i // RANK, i % RANK]
-            dup[i // RANK, i % RANK] = jnp.concatenate([x, x], axis=1)
-            return 0
-
-        lax.fori_loop(0, 4 * RANK, block, 0, unroll=8)
-
-    doubled(u_raw, u_dup)
-
-    def roots():
-        total = jnp.zeros((RANK, 128), F32)
-        for px in range(4):
-            total = row_products(total, ctf.at[px], u_dup, px)
-        return total
-
-    ring = send_roots(0, roots())
+    tiles_load.wait()
+    tile_copy = remote(tcx.at[:, :, owner], tcx.at[:, :, owner], one_send.at[1], one_recv.at[1], {"owner": 1 - owner})
+    tile_copy.start()
+
+    lk_load.wait()
+    prepare_masks()
+    lt_load.wait()
+    prepare_leaf_tiles()
+    upc_load.wait()
+    prepare_coarse()
+    reach = send_groups(0, ring)
 
     for s in range(2):
         for t in range(4):
@@ -387,47 +403,41 @@
         copy.wait()
     others.wait_recv()
     lax.fori_loop(0, 4, reaction, 0)
-
-    reach = send_groups(0, ring)
     for copy in halos:
         copy.wait_recv()
     edge.wait_recv()
     lax.fori_loop(0, 2, advection, 0)
     nb_load.wait()
-    near(0)
+    near(0, (0, 1, 2, 3))
     eye = rows((256, 256)) == lanes((256, 256))
     diag = jnp.sum(jnp.where(eye, nb[4].astype(F32), 0.0), axis=0, keepdims=True)
     inverse_diag = 1.0 / (1.0 + scale * diag)
-    lk_load.wait()
-    prepare_masks()
-    lt_load.wait()
-    prepare_leaf_tiles()
     leaf(0)
-    upc_load.wait()
     tile_copy.wait_recv()
-    prepare_coarse()
+    prepare_coarse_tiles()
     for copy in d_loads:
         copy.wait()
-    doubled(d_raw, d_dup)
     for copy in reach:
         copy.wait_recv()
     coarse(0)
-    finish(0, s0, cur, inverse_diag)
+    finish(s0, cur, inverse_diag)
 
     own_columns(1, cur)
     halos_1 = halo_copies(1)
+    p1[1, 0] = root_tile(roots())
+    ring_1 = send_roots(1)
     for copy in halos_1:
         copy.start()
-    ring_1 = send_roots(1, roots())
+    near(1, (1, 2))
+    reach_1 = send_groups(1, ring_1)
     for copy in halos_1:
         copy.wait_recv()
-    near(1)
-    reach_1 = send_groups(1, ring_1)
+    near(1, (0, 3))
     leaf(1)
     for copy in reach_1:
         copy.wait_recv()
     coarse(1)
-    finish(1, cur, out, inverse_diag)
+    finish(cur, out, inverse_diag)
 
     for copy in halos + halos_1 + [others, tile_copy, edge] + ring + ring_1 + reach + reach_1:
         copy.wait_send()
@@ -448,9 +458,8 @@
         pltpu.VMEM((4, 128, 256), F32),
         pltpu.VMEM((2, 6, 128, 256), BF16),
         pltpu.VMEM((4, 128, 256), BF16),
-        pltpu.VMEM((4, RANK, 128), F32),
+        pltpu.VMEM((2, 4, RANK, 64), F32),
         pltpu.VMEM((2, 10, RANK, 128), BF16),
-        pltpu.VMEM((10, RANK, 128), F32),
         pltpu.VMEM((2, 5, 64, 256), F32),
         pltpu.VMEM((2, 4, 64, 256), F32),
         pltpu.VMEM((2, 4, 64, 256), I32),
@@ -460,28 +469,26 @@
         pltpu.VMEM((40, RANK, RANK), F32),
         pltpu.VMEM((RANK, 40 * RANK), BF16),
         pltpu.VMEM((4, 40, 64), I32),
-        pltpu.VMEM((4, 40, 128), F32),
-        pltpu.VMEM((4, 7 * RANK, 128), BF16),
+        pltpu.VMEM((4, 40, 16, 128), BF16),
+        pltpu.VMEM((2, 7 * RANK, 512), BF16),
         pltpu.VMEM((4, RANK, RANK, 64), F32),
-        pltpu.VMEM((4, RANK, RANK, 128), F32),
         pltpu.VMEM((4, RANK, RANK, 64), F32),
-        pltpu.VMEM((4, RANK, RANK, 128), F32),
         pltpu.VMEM((2, RANK, RANK, 64), F32),
         pltpu.VMEM((2, RANK, RANK, 128), F32),
         pltpu.VMEM((3, 4, 2, 24, RANK), F32),
-        pltpu.VMEM((RANK, 12 * RANK), F32),
+        pltpu.VMEM((2, RANK, 12 * 64), BF16),
         pltpu.VMEM((8, 128), F32),
-        pltpu.VMEM((RANK, 128), F32),
-        pltpu.VMEM((RANK, 128), F32),
+        pltpu.VMEM((2, RANK, 64), F32),
         pltpu.VMEM((4, RANK, 128), F32),
-        pltpu.VMEM((2, 8, 8, 128), F32),
-        pltpu.VMEM((2, 16, 8, 128), F32),
+        pltpu.VMEM((4, RANK, 128), BF16),
+        pltpu.VMEM((2, 4, 8, 128), F32),
+        pltpu.VMEM((2, 2, 16, 8, 128), F32),
         dma((14,)),
         dma((4, 8)),
-        dma((2, 8)),
-        dma((2, 8)),
-        dma((2, 7)),
-        dma((2, 7)),
+        dma((2, 4)),
+        dma((2, 4)),
+        dma((2, 13)),
+        dma((2, 13)),
         dma((2, 4)),
         dma((2, 4)),
         dma((3,)),
@@ -489,7 +496,7 @@
     ]
     result = pl.pallas_call(
         kernel,
-        out_shape=jax.ShapeDtypeStruct((4, 128, 256), F32),
+        out_shape=pltpu.VMEM((4, 128, 256), F32),
         in_specs=[anywhere] * 12 + [vmem, smem, smem],
         out_specs=vmem,
         scratch_shapes=scratch,

time: 53.1 us -> 39.5 us (0.74)
  Pallas kernels: 50.6 us -> 38.3 us
  local copies, waits for them, and re-layouts: 2.17 us -> 1.13 us
    pallas_call x1, Pallas kernels: 50.6 us -> 38.3 us  [per_device(): pl.pallas_call(kernel, out_shape=pltpu.VMEM((4, 128, 256), F32), in_specs...]
    reshape x1, local copies, waits for them, and re-layouts: 2.17 us -> 1.13 us  [per_device(): return jnp.transpose(result.reshape(4, 2, PY, 256), (1, 2, 0, 3))]
where the time goes in v1:
time: 39.5 us; the launch traced here: 39.4 us
  Pallas kernels  38.3 us (97%)
  local copies, waits for them, and re-layouts  1.13 us (3%)
    pallas_call x1, Pallas kernels, per_device(): pl.pallas_call(kernel, out_shape=pltpu.VMEM((4, 128, 256), F32), in_specs...  38.3 us
    reshape x1, local copies, waits for them, and re-layouts, per_device(): return jnp.transpose(result.reshape(4, 2, PY, 256), (1, 2, 0, 3))  1.13 us

profile of v1, /device:TPU:2, one launch (start us, length us, event | category | flops | bytes accessed | tf_op | source)
XLA Modules:
  0.0 39.4 jit_solution(14282632263440038174)
XLA Ops:
  0.0 38.3 %shard_map.145 = f32[4,128,256]{2,1,0:T(8,128)S(1)} custom-call(f32[2,64,4,256]{3,2,1,0:T(4,128)} %state.1, bf16[9,256,256]{2,1,0:T(8,128)(2,1)} %near_blocks.1, bf16[48,256]{1,0:T(8,128)(2,1)} %bitcast.19, f32[40,48,48]{2,1,0:T(8,128)} %leaf_tiles.1, s32[4,40,64]{2,1,0:T(8,128)} %bitcast.18, f32[4,48,48,64]{3,2,1,0:T(8,128)} %bitcast.14, ...), custom_call_target="tpu_custom_call" | custom-call | tf_op jit(solution)/shard_map/pallas_call | solution.py:497
  38.3 1.1 %copy.18 = f32[4,2,64,256]{3,0,2,1:T(4,128)} copy(f32[4,2,64,256]{3,2,1,0:T(8,128)S(1)} %bitcast.13) | data formatting | bytes 1048576 | tf_op jit(solution)/shard_map/reshape | solution.py:523

commit v2 on v1

--- a/solution.py
+++ b/solution.py
@@ -69,7 +69,7 @@
     rate, coarse_links, diffusion,
     out,
     s0, cur, tgt, near_acc, low, oth, ctf, ctb, q, spd, upw, zon, nb, bt, lt, ltt, lk, msk, rhs,
-    u_raw, d_raw, upc, upg, tcx, t2, tab, cfb, expd, fld, p1, r2,
+    u_raw, u_wide, d_raw, d_wide, ctw, upc, upg, tcx, t2, tab, cfb, expd, fld, p1, r2,
     load_sem, load8_sem, p1_send, p1_recv, r2_send, r2_recv, halo_send, halo_recv, one_send, one_recv,
 ):
     cluster = lax.axis_index("cluster")
@@ -119,18 +119,6 @@
                 copy = pltpu.make_async_copy(src.at[e, :, px], dst.at[e, px], load8_sem.at[1 + j, e * 4 + px])
                 copy.start()
                 flow_loads.append(copy)
-    tiles_load = load(tiles, tcx.at[:, :, owner], 5)
-    lk_load = load(links, lk, 7)
-    upc_load = load(up_coarse, upc, 8)
-    lt_load = load(leaf_tiles, lt, 9)
-    zone_loads = []
-    for px in range(4):
-        copy = pltpu.make_async_copy(zone.at[:, px], zon.at[px], load8_sem.at[3, px])
-        copy.start()
-        zone_loads.append(copy)
-    nb_load = load(near_blocks, nb, 6)
-    d_loads = [load(down_leaf.at[px], d_raw.at[px], 10 + px) for px in range(4)]
-
     def remote(src, dst, send, recv, device_id):
         return pltpu.make_async_remote_copy(
             src_ref=src, dst_ref=dst, send_sem=send, recv_sem=recv,
@@ -148,8 +136,14 @@
             v = src[px].astype(BF16)
             low[k, px + 1] = v
             coeffs = dot(bt[...], v, NT)
-            ctf[0, px] = coeffs[:, :64]
-            ctf[1, px] = coeffs[:, 64:]
+            if k == 0:
+                ctf[0, px] = coeffs[:, :64]
+                ctf[1, px] = coeffs[:, 64:]
+            elif px % 2 == 0:
+                even = coeffs
+            else:
+                ctw[0, px // 2] = jnp.concatenate([even[:, :64], coeffs[:, :64]], axis=1)
+                ctw[1, px // 2] = jnp.concatenate([even[:, 64:], coeffs[:, 64:]], axis=1)
             ctb[k, px + 3] = coeffs.astype(BF16)
 
     def halo_copies(k):
@@ -161,11 +155,13 @@
             remote(ctb.at[k, pl.ds(3, 3)], ctb.at[k, pl.ds(7, 3)], h.at[k, 3], g.at[k, 3], left_id),
         ]
 
-    def root_tile(total):
-        pick_row = rows((8, 128)) - 2 * y0
-        pick = jnp.where((pick_row >= 0) & (pick_row < 2) & (lanes((8, 128)) // 64 == pick_row), 1.0, 0.0).astype(BF16)
-        padded = jnp.concatenate([total, jnp.zeros((128 - RANK, 128), F32)], axis=0)
-        return split_dot(pick, padded, NT, 0)
+    def root_tile(totals):
+        total = jnp.concatenate(totals, axis=1)
+        width = total.shape[1]
+        pick_row = rows((8, width)) - 2 * y0
+        mine = (pick_row >= 0) & (pick_row < 2) & (lanes((8, width)) // (width // 2) == pick_row)
+        padded = jnp.concatenate([total, jnp.zeros((128 - RANK, width), F32)], axis=0)
+        return split_dot(jnp.where(mine, 1.0, 0.0).astype(BF16), padded, NT, 0)
 
     def send_roots(k):
         copies = [remote(p1.at[k, 0], p1.at[k, j], p1_send.at[k, j], p1_recv.at[k, j], ring_id(j)) for j in (2, 1, 3)]
@@ -252,12 +248,9 @@
         for i, target in enumerate(((4 * at_group + at_y) % n_clusters, (2 * at_group + at_y // 2) % (n_clusters // 2))):
             pick = jnp.where((rows((64, 128)) == target) & (lane < 56), 1.0, 0.0).astype(BF16)
 
-            def block(b, _, pick=pick, i=i):
-                x = upc[i, pl.ds(b * 8, 8)].reshape(8 * RANK, 64).astype(BF16)
-                upg[i, pl.ds(b * 8, 8)] = dot(x, pick, NN).reshape(8, RANK, 128)
-                return 0
-
-            lax.fori_loop(0, RANK // 8, block, 0)
+            for r in range(0, RANK, 8):
+                x = upc[i, r : r + 8].reshape(8 * RANK, 64).astype(BF16)
+                upg[i, r : r + 8] = dot(x, pick, NN).reshape(8, RANK, 128)
     def prepare_coarse_tiles():
         t2[...] = jnp.zeros_like(t2)
         for l in range(3):
@@ -297,21 +290,30 @@
         found = dot(t2[0], high, NN) + (dot(t2[0], rest, NN) + dot(t2[1], high, NN))
         spread = jnp.where(rows((128, 256)) % 2 == lanes((128, 256)) // 128, 1.0, 0.0).astype(BF16)
         both = split_dot(found, spread, NN, 1)
-        cfb[0] = both[:, :64]
-        cfb[1] = both[:, 128:192]
-
-    def finish(src, dst, inverse_diag):
-        def expand(px, _):
-            zero = jnp.zeros((RANK, 64), F32)
-            expanded = both_products((zero, zero), (cfb[0], cfb[1]), d_raw, px)
-            fld[px] = (expd[px] + jnp.concatenate(expanded, axis=1)).astype(BF16)
+        cfb[0] = both[:, :128]
+        cfb[1] = both[:, 128:]
+
+    def expand(j, _):
+        zero = jnp.zeros((RANK, 128), F32)
+        e0, e1 = both_products((zero, zero), (cfb[0], cfb[1]), d_wide, j)
+        for i in range(2):
+            half = slice(64 * i, 64 * i + 64)
+            expanded = jnp.concatenate([e0[:, half], e1[:, half]], axis=1)
+            fld[2 * j + i] = (expd[2 * j + i] + expanded).astype(BF16)
+        return 0
+
+    def prepare_finish(src, inverse_diag):
+        def column(px, _):
+            v = src[px]
+            near_acc[px] = v + (tgt[px] - v - scale * near_acc[px]) * inverse_diag
             return 0
 
-        lax.fori_loop(0, 4, expand, 0)
+        lax.fori_loop(0, 4, column, 0)
+
+    def finish(dst, weight):
+        lax.fori_loop(0, 2, expand, 0)
         for px in range(4):
-            applied = near_acc[px] + dot(fld[px], bt[...], TN)
-            v = src[px]
-            dst[px] = v + (tgt[px] - v - scale * applied) * inverse_diag
+            dst[px] = near_acc[px] - weight * dot(fld[px], bt[...], TN)
 
     def reaction(px, _):
         z = zon[px]
@@ -356,12 +358,38 @@
     own_columns(0, s0)
     for copy in u_loads:
         copy.wait()
+    tiles_load = load(tiles, tcx.at[:, :, owner], 5)
+    lk_load = load(links, lk, 7)
+    upc_load = load(up_coarse, upc, 8)
+    lt_load = load(leaf_tiles, lt, 9)
+    zone_loads = []
+    for px in range(4):
+        copy = pltpu.make_async_copy(zone.at[:, px], zon.at[px], load8_sem.at[3, px])
+        copy.start()
+        zone_loads.append(copy)
+    nb_load = load(near_blocks, nb, 6)
+    d_loads = [load(down_leaf.at[px], d_raw.at[px], 10 + px) for px in range(4)]
+
 
     def roots():
         totals = lax.fori_loop(
             0, 4, lambda px, t: both_products(t, (ctf[0, px], ctf[1, px]), u_raw, px), (jnp.zeros((RANK, 64), F32),) * 2
         )
-        return jnp.concatenate(totals, axis=1)
+        return totals
+
+    def wide_roots():
+        zero = jnp.zeros((RANK, 128), F32)
+        return lax.fori_loop(
+            0, 2, lambda j, t: both_products(t, (ctw[0, j], ctw[1, j]), u_wide, j), (zero, zero)
+        )
+
+    def pack(raw, wide):
+        def pair(j, _):
+            for r in range(RANK):
+                wide[j, r] = jnp.concatenate([raw[2 * j, r], raw[2 * j + 1, r]], axis=1)
+            return 0
+
+        lax.fori_loop(0, 2, pair, 0)
 
     p1[0, 0] = root_tile(roots())
     pl.semaphore_wait(barrier, len(partners))
@@ -412,19 +440,23 @@
     eye = rows((256, 256)) == lanes((256, 256))
     diag = jnp.sum(jnp.where(eye, nb[4].astype(F32), 0.0), axis=0, keepdims=True)
     inverse_diag = 1.0 / (1.0 + scale * diag)
+    weight = scale * inverse_diag
     leaf(0)
     tile_copy.wait_recv()
     prepare_coarse_tiles()
+    pack(u_raw, u_wide)
     for copy in d_loads:
         copy.wait()
+    pack(d_raw, d_wide)
+    prepare_finish(s0, inverse_diag)
     for copy in reach:
         copy.wait_recv()
     coarse(0)
-    finish(s0, cur, inverse_diag)
+    finish(cur, weight)
 
     own_columns(1, cur)
     halos_1 = halo_copies(1)
-    p1[1, 0] = root_tile(roots())
+    p1[1, 0] = root_tile(wide_roots())
     ring_1 = send_roots(1)
     for copy in halos_1:
         copy.start()
@@ -434,10 +466,11 @@
         copy.wait_recv()
     near(1, (0, 3))
     leaf(1)
+    prepare_finish(cur, inverse_diag)
     for copy in reach_1:
         copy.wait_recv()
     coarse(1)
-    finish(cur, out, inverse_diag)
+    finish(out, weight)
 
     for copy in halos + halos_1 + [others, tile_copy, edge] + ring + ring_1 + reach + reach_1:
         copy.wait_send()
@@ -472,13 +505,16 @@
         pltpu.VMEM((4, 40, 16, 128), BF16),
         pltpu.VMEM((2, 7 * RANK, 512), BF16),
         pltpu.VMEM((4, RANK, RANK, 64), F32),
+        pltpu.VMEM((2, RANK, RANK, 128), F32),
         pltpu.VMEM((4, RANK, RANK, 64), F32),
+        pltpu.VMEM((2, RANK, RANK, 128), F32),
+        pltpu.VMEM((2, 2, RANK, 128), F32),
         pltpu.VMEM((2, RANK, RANK, 64), F32),
         pltpu.VMEM((2, RANK, RANK, 128), F32),
         pltpu.VMEM((3, 4, 2, 24, RANK), F32),
         pltpu.VMEM((2, RANK, 12 * 64), BF16),
         pltpu.VMEM((8, 128), F32),
-        pltpu.VMEM((2, RANK, 64), F32),
+        pltpu.VMEM((2, RANK, 128), F32),
         pltpu.VMEM((4, RANK, 128), F32),
         pltpu.VMEM((4, RANK, 128), BF16),
         pltpu.VMEM((2, 4, 8, 128), F32),

time: 39.5 us -> 39.8 us (level)
  no operation moved by 1% of the time
where the time goes in v2:
time: 39.8 us; the launch traced here: 39.6 us
  Pallas kernels  38.5 us (97%)
  local copies, waits for them, and re-layouts  1.13 us (3%)
    pallas_call x1, Pallas kernels, per_device(): pl.pallas_call(kernel, out_shape=pltpu.VMEM((4, 128, 256), F32), in_specs...  38.5 us
    reshape x1, local copies, waits for them, and re-layouts, per_device(): return jnp.transpose(result.reshape(4, 2, PY, 256), (1, 2, 0, 3))  1.13 us

profile of v2, /device:TPU:2, one launch (start us, length us, event | category | flops | bytes accessed | tf_op | source)
XLA Modules:
  0.0 39.6 jit_solution(17374641911523502776)
XLA Ops:
  0.0 38.5 %shard_map.145 = f32[4,128,256]{2,1,0:T(8,128)S(1)} custom-call(f32[2,64,4,256]{3,2,1,0:T(4,128)} %state.1, bf16[9,256,256]{2,1,0:T(8,128)(2,1)} %near_blocks.1, bf16[48,256]{1,0:T(8,128)(2,1)} %bitcast.19, f32[40,48,48]{2,1,0:T(8,128)} %leaf_tiles.1, s32[4,40,64]{2,1,0:T(8,128)} %bitcast.18, f32[4,48,48,64]{3,2,1,0:T(8,128)} %bitcast.14, ...), custom_call_target="tpu_custom_call" | custom-call | tf_op jit(solution)/shard_map/pallas_call | solution.py:533
  38.5 1.1 %copy.18 = f32[4,2,64,256]{3,0,2,1:T(4,128)} copy(f32[4,2,64,256]{3,2,1,0:T(8,128)S(1)} %bitcast.13) | data formatting | bytes 1048576 | tf_op jit(solution)/shard_map/reshape | solution.py:559

commit v3 on v2

--- a/solution.py
+++ b/solution.py
@@ -362,13 +362,13 @@
     lk_load = load(links, lk, 7)
     upc_load = load(up_coarse, upc, 8)
     lt_load = load(leaf_tiles, lt, 9)
+    d_loads = [load(down_leaf.at[px], d_raw.at[px], 10 + px) for px in range(4)]
     zone_loads = []
     for px in range(4):
         copy = pltpu.make_async_copy(zone.at[:, px], zon.at[px], load8_sem.at[3, px])
         copy.start()
         zone_loads.append(copy)
     nb_load = load(near_blocks, nb, 6)
-    d_loads = [load(down_leaf.at[px], d_raw.at[px], 10 + px) for px in range(4)]
 
 
     def roots():
@@ -421,6 +421,10 @@
     prepare_leaf_tiles()
     upc_load.wait()
     prepare_coarse()
+    pack(u_raw, u_wide)
+    for copy in d_loads:
+        copy.wait()
+    pack(d_raw, d_wide)
     reach = send_groups(0, ring)
 
     for s in range(2):
@@ -444,10 +448,6 @@
     leaf(0)
     tile_copy.wait_recv()
     prepare_coarse_tiles()
-    pack(u_raw, u_wide)
-    for copy in d_loads:
-        copy.wait()
-    pack(d_raw, d_wide)
     prepare_finish(s0, inverse_diag)
     for copy in reach:
         copy.wait_recv()

time: 39.8 us -> 38.3 us (0.962)
  Pallas kernels: 38.5 us -> 37 us
    pallas_call x1, Pallas kernels: 38.5 us -> 37 us  [per_device(): pl.pallas_call(kernel, out_shape=pltpu.VMEM((4, 128, 256), F32), in_specs...]
where the time goes in v3:
time: 38.3 us; the launch traced here: 38.2 us
  Pallas kernels  37 us (97%)
  local copies, waits for them, and re-layouts  1.13 us (3%)
    pallas_call x1, Pallas kernels, per_device(): pl.pallas_call(kernel, out_shape=pltpu.VMEM((4, 128, 256), F32), in_specs...  37 us
    reshape x1, local copies, waits for them, and re-layouts, per_device(): return jnp.transpose(result.reshape(4, 2, PY, 256), (1, 2, 0, 3))  1.13 us

profile of v3, /device:TPU:2, one launch (start us, length us, event | category | flops | bytes accessed | tf_op | source)
XLA Modules:
  0.0 38.2 jit_solution(10166947959216397995)
XLA Ops:
  0.0 37.0 %shard_map.145 = f32[4,128,256]{2,1,0:T(8,128)S(1)} custom-call(f32[2,64,4,256]{3,2,1,0:T(4,128)} %state.1, bf16[9,256,256]{2,1,0:T(8,128)(2,1)} %near_blocks.1, bf16[48,256]{1,0:T(8,128)(2,1)} %bitcast.19, f32[40,48,48]{2,1,0:T(8,128)} %leaf_tiles.1, s32[4,40,64]{2,1,0:T(8,128)} %bitcast.18, f32[4,48,48,64]{3,2,1,0:T(8,128)} %bitcast.14, ...), custom_call_target="tpu_custom_call" | custom-call | tf_op jit(solution)/shard_map/pallas_call | solution.py:533
  37.0 1.1 %copy.18 = f32[4,2,64,256]{3,0,2,1:T(4,128)} copy(f32[4,2,64,256]{3,2,1,0:T(8,128)S(1)} %bitcast.13) | data formatting | bytes 1048576 | tf_op jit(solution)/shard_map/reshape | solution.py:559
